TPU v7x, 32 devices: a whole 2x2x4 slice. The times are simulated.
32 devices in a mesh: grp: 2 (over y), row: 4 (over x, core), col: 4 (over z).
Axes of the slice: x: 2, y: 2, z: 4, core: 2. Of those that a mesh axis runs over, the one named last changes fastest.
Arguments:
- object_field: float32 [4, 2, 1024, 1024], P('grp', None, 'row', 'col'), parts along dimension 0, may hold values from -4.2 to 4.2
- probe_modes: float32 [6, 2, 256, 256], P('grp'), parts along dimension 0, may hold values from -2.4 to 2.4
- measured: float32 [8, 4, 2, 256, 256], P(('grp', 'row'), 'col'), parts along dimension 0, may hold values from 0.2 to 3
- offsets: int32 [8, 4, 2, 2], P(('grp', 'row'), 'col'), parts along dimension 0, may hold values from -64 to 64, as said below
Outputs:
- object_grad: float32 [4, 2, 1024, 1024], P('grp', None, 'row', 'col'), parts along dimension 0
- new_probe: float32 [6, 2, 256, 256], P('grp'), parts along dimension 0
There are 2 independent parts, one for each index of `grp`. A program takes and returns all parts, laid end to end along the dimension named above; each array names one. Nothing has to cross between parts.
Inputs may be any that keep to these rules, and one draw needn't show every extreme that they name: Windows of the first and last tile rows and columns stay inside the object; a tile's row offsets reach at most 64 and its column offsets at most 64.
All inputs are finite; a program needn't handle non-finite values.
Results may differ from a plain program's by a relative error of at most 0.00013.
Values sent between devices are 32-bit elements; how exact they have to be, the bound alone decides.
A program may use at most 128 MiB of HBM per device.

v0:
```python
import functools
import math

import jax
import jax.numpy as jnp
import numpy as np
from jax import lax
from jax.experimental import pallas as pl
from jax.experimental.pallas import tpu as pltpu
from jax.sharding import PartitionSpec as P

HALO = 64
EPSILON = 1e-06
PROP_PHASE = 40.0


def shifted(block, axis, distance):
    devices = range(lax.axis_size(axis))
    route = [(i - distance, i) for i in devices if i - distance in devices]
    return lax.ppermute(block, axis, route)


def with_halo(block, sides, width):
    for axis, dim in sides:
        count = lax.axis_size(axis)
        forward = [(i, i + 1) for i in range(count - 1)]
        backward = [(target, source) for source, target in forward]
        low = lax.ppermute(
            lax.slice_in_dim(block, block.shape[dim] - width, None, axis=dim), axis, forward
        )
        high = lax.ppermute(lax.slice_in_dim(block, 0, width, axis=dim), axis, backward)
        block = jnp.concatenate([low, block, high], axis=dim)
    return block


def split_tables(size):
    index = np.arange(size)
    turn = (index[:, None] * index[None, :]) % size
    dft = np.exp(-2j * np.pi * turn / size) / math.sqrt(size)
    freq = ((index + size // 2) % size - size // 2) / size
    prop = np.conj(dft) @ (np.exp(-1j * PROP_PHASE * freq**2)[:, None] * dft)
    stacked = []
    for matrix in (dft, prop):
        for part in (matrix.real, matrix.imag - matrix.real, matrix.imag + matrix.real):
            high = part.astype(jnp.bfloat16)
            low = (part - high.astype(np.float64)).astype(jnp.bfloat16)
            stacked.append(np.stack([high, low]))
    return np.stack(stacked)


def split(value):
    high = value.astype(jnp.bfloat16)
    return high, (value - high.astype(jnp.float32)).astype(jnp.bfloat16)


def mul_right(value, tab, k):
    high, low = split(value)
    t_high, t_low = tab[k, 0], tab[k, 1]
    return jnp.dot(
        jnp.concatenate([high, low, high], axis=1),
        jnp.concatenate([t_high, t_high, t_low], axis=0),
        preferred_element_type=jnp.float32,
    )


def mul_left(value, tab, k):
    high, low = split(value)
    t_high, t_low = tab[k, 0], tab[k, 1]
    return jnp.dot(
        jnp.concatenate([t_high, t_high, t_low], axis=1),
        jnp.concatenate([high, low, high], axis=0),
        preferred_element_type=jnp.float32,
    )


def both_sides(re, im, tab, base, conj):
    for mul in (mul_right, mul_left):
        both = mul(re + im, tab, base)
        if conj:
            re, im = both + mul(im, tab, base + 1), both - mul(re, tab, base + 2)
        else:
            re, im = both - mul(im, tab, base + 2), both + mul(re, tab, base + 1)
    return re, im


def gradient_kernel(offs, ext, probe, meas, tab, grad, pgrad, win, wave, far, inten, terms):
    modes, size = probe.shape[0], probe.shape[2]
    layers, wide = ext.shape[0], ext.shape[3]
    positions = meas.shape[2]
    grad[...] = jnp.zeros_like(grad)
    pgrad[...] = jnp.zeros_like(pgrad)

    def position(p, carry):
        row = offs[0, 0, p, 0] + HALO
        col = offs[0, 0, p, 1] + HALO
        base = pl.multiple_of(jnp.minimum(row // 8, (2 * HALO - 8) // 8) * 8, 8)
        rest = row - base
        tall = size + 8
        for l in range(layers):
            for c in range(2):
                rows = ext[l, c, pl.ds(base, tall), :]
                rows = pltpu.roll(rows, lax.rem(wide - col, wide), 1)[:, :size]
                win[l, c] = pltpu.roll(rows, lax.rem(tall - rest, tall), 0)[:size]
        inten[...] = -meas[0, 0, p]
        terms[...] = jnp.zeros_like(terms)
        last = layers - 1

        def forward(m, carry):
            re, im = probe[m, 0], probe[m, 1]
            for l in range(layers):
                t_re, t_im = win[l, 0], win[l, 1]
                e_re = t_re * re - t_im * im
                e_im = t_re * im + t_im * re
                if l < last:
                    re, im = both_sides(e_re, e_im, tab, 3, False)
                    wave[l, m, 0] = re
                    wave[l, m, 1] = im
                else:
                    re, im = both_sides(e_re, e_im, tab, 0, False)
            far[m, 0] = re
            far[m, 1] = im
            inten[...] += re * re + im * im
            return carry

        lax.fori_loop(0, modes, forward, 0, unroll=UNROLL)

        def backward(m, carry):
            misfit = inten[...]
            re, im = both_sides(misfit * far[m, 0], misfit * far[m, 1], tab, 0, True)
            for l in range(last, -1, -1):
                w_re = wave[l - 1, m, 0] if l > 0 else probe[m, 0]
                w_im = wave[l - 1, m, 1] if l > 0 else probe[m, 1]
                terms[l, 0] += w_re * re + w_im * im
                terms[l, 1] += w_re * im - w_im * re
                t_re, t_im = win[l, 0], win[l, 1]
                b_re = t_re * re + t_im * im
                b_im = t_re * im - t_im * re
                if l > 0:
                    re, im = both_sides(b_re, b_im, tab, 3, True)
                else:
                    pgrad[m, 0] += b_re
                    pgrad[m, 1] += b_im
            return carry

        lax.fori_loop(0, modes, backward, 0, unroll=UNROLL)
        for l in range(layers):
            for c in range(2):
                padded = jnp.concatenate([terms[l, c], jnp.zeros((8, size), jnp.float32)], axis=0)
                padded = pltpu.roll(padded, rest, 0)
                padded = jnp.concatenate(
                    [padded, jnp.zeros((tall, wide - size), jnp.float32)], axis=1
                )
                grad[l, c, pl.ds(base, tall), :] += pltpu.roll(padded, col, 1)
        return carry

    lax.fori_loop(0, positions, position, 0)


UNROLL = True


def total(value):
    return jnp.sum(jnp.sum(value, axis=0, keepdims=True), axis=1, keepdims=True)


def update_modes(probe, summed, out):
    modes = probe.shape[0]
    probe_sq = total(sum(probe[m, c] * probe[m, c] for m in range(modes) for c in range(2)))
    grad_sq = total(sum(summed[m, c] * summed[m, c] for m in range(modes) for c in range(2)))
    factor = 0.5 * jnp.sqrt(probe_sq / (grad_sq + EPSILON))
    norms = []
    for k in range(modes):
        out[k, 0] = probe[k, 0] - factor * summed[k, 0]
        out[k, 1] = probe[k, 1] - factor * summed[k, 1]
        ratios = []
        for a in range(k):
            inner_re = total(out[a, 0] * out[k, 0] + out[a, 1] * out[k, 1])
            inner_im = total(out[a, 0] * out[k, 1] - out[a, 1] * out[k, 0])
            ratios.append((inner_re / norms[a], inner_im / norms[a]))
        if k:
            re, im = out[k, 0], out[k, 1]
            for a, (r_re, r_im) in enumerate(ratios):
                re = re - (r_re * out[a, 0] - r_im * out[a, 1])
                im = im - (r_re * out[a, 1] + r_im * out[a, 0])
            out[k, 0] = re
            out[k, 1] = im
        norms.append(total(out[k, 0] * out[k, 0] + out[k, 1] * out[k, 1]) + EPSILON)


def gradients(offsets, extended, probe_modes, measured):
    modes, _, size, _ = probe_modes.shape
    layers = extended.shape[0]
    vmem = pl.BlockSpec(memory_space=pltpu.VMEM)
    f32 = jnp.float32
    tables = jnp.asarray(split_tables(size))
    return pl.pallas_call(
        gradient_kernel,
        out_shape=(
            jax.ShapeDtypeStruct(extended.shape, f32),
            jax.ShapeDtypeStruct(probe_modes.shape, f32),
        ),
        in_specs=[pl.BlockSpec(memory_space=pltpu.SMEM), vmem, vmem, vmem, vmem],
        out_specs=(vmem, vmem),
        scratch_shapes=[
            pltpu.VMEM((layers, 2, size, size), f32),
            pltpu.VMEM((max(layers - 1, 1), modes, 2, size, size), f32),
            pltpu.VMEM((modes, 2, size, size), f32),
            pltpu.VMEM((size, size), f32),
            pltpu.VMEM((layers, 2, size, size), f32),
        ],
        compiler_params=pltpu.CompilerParams(vmem_limit_bytes=48 << 20),
    )(offsets, extended, probe_modes, measured, tables)


def new_modes(probe_modes, summed):
    return pl.pallas_call(
        update_modes,
        out_shape=jax.ShapeDtypeStruct(probe_modes.shape, jnp.float32),
        compiler_params=pltpu.CompilerParams(vmem_limit_bytes=32 << 20),
    )(probe_modes, summed)


def fold(edge_grad, axis, dim):
    count = edge_grad.shape[dim]
    cut = functools.partial(lax.slice_in_dim, edge_grad, axis=dim)
    from_high = shifted(cut(0, HALO), axis, -1)
    from_low = shifted(cut(count - HALO, count), axis, 1)
    return jnp.concatenate(
        [
            cut(HALO, 2 * HALO) + from_low,
            cut(2 * HALO, count - 2 * HALO),
            cut(count - 2 * HALO, count - HALO) + from_high,
        ],
        axis=dim,
    )


def shards(object_field, probe_modes, measured, offsets):
    extended = with_halo(object_field, (("row", 2), ("col", 3)), HALO)
    grad_ext, local_grad = gradients(offsets, extended, probe_modes, measured)
    summed = lax.psum(local_grad, ("row", "col"))
    object_grad = fold(fold(grad_ext, "row", 2), "col", 3)
    return (object_grad, new_modes(probe_modes, summed))


def solution(mesh):
    placed = (
        P("grp", None, "row", "col"),
        P("grp", None, None, None),
        P(("grp", "row"), "col", None, None, None),
        P(("grp", "row"), "col", None, None),
    )
    return jax.shard_map(
        shards,
        mesh=mesh,
        in_specs=placed,
        out_specs=(P("grp", None, "row", "col"), P("grp", None, None, None)),
        check_vma=False,
    )
```

profile of v0, /device:TPU:0, one launch (start us, length us, event | category | flops | bytes accessed | tf_op | source)
XLA Modules:
  0.0 201.8 jit_solution(17260858535093803904)
XLA Ops:
  8.4 2.4 %collective-permute-start = (f32[2,2,64,256]{3,2,1,0:T(8,128)S(1)}, f32[2,2,64,256]{3,2,1,0:T(8,128)S(1)}, u32[]{:S(2)}, u32[]{:S(2)}) collective-permute-start(f32[2,2,64,256]{3,2,1,0:T(8,128)S(1)} %get-tuple-element.13), channel_id=1, source_target_pairs={{0,4},{4,8},{8,12},{1,5},{5,9},{9,13},{2,6},{6,10},{10,14},{3,7},{... | collective-permute-start | bytes 786440 | tf_op jit(solution)/shard_map/ppermute | solution.py:28
  10.8 1.3 collective-permute-start.1
  12.2 4.1 %collective-permute-done.1 = f32[2,2,64,256]{3,2,1,0:T(8,128)S(1)} collective-permute-done((f32[2,2,64,256]{3,2,1,0:T(8,128)S(1)}, f32[2,2,64,256]{3,2,1,0:T(8,128)S(1)}, u32[]{:S(2)}, u32[]{:S(2)}) %collective-permute-start.1) | collective-permute-done | bytes 262176 | tf_op jit(solution)/shard_map/ppermute | solution.py:31
  16.8 1.3 collective-permute-start.3
  18.4 4.6 %collective-permute-start.2 = (f32[2,2,384,64]{2,3,1,0:T(8,128)S(1)}, f32[2,2,384,64]{2,3,1,0:T(8,128)S(1)}, u32[]{:S(2)}, u32[]{:S(2)}) collective-permute-start(f32[2,2,384,64]{2,3,1,0:T(8,128)S(1)} %copy.7), channel_id=1, source_target_pairs={{0,1},{1,2},{2,3},{4,5},{5,6},{6,7},{8,9},{9,10},{10,11},{12,13},{... | collective-permute-start | bytes 1179656 | tf_op jit(solution)/shard_map/ppermute | solution.py:28
  23.0 3.9 %collective-permute-done.3 = f32[2,2,384,64]{2,3,1,0:T(8,128)S(1)} collective-permute-done((f32[2,2,384,64]{2,3,1,0:T(8,128)S(1)}, f32[2,2,384,64]{2,3,1,0:T(8,128)S(1)}, u32[]{:S(2)}, u32[]{:S(2)}) %collective-permute-start.3) | collective-permute-done | bytes 393248 | tf_op jit(solution)/shard_map/ppermute | solution.py:31
  26.9 1.2 copy.10
  28.8 1.2 copy.9
  30.0 3.8 %pad_maximum_fusion.ext = f32[2,2,384,384]{3,2,1,0:T(8,128)} fusion(f32[2,2,384,64]{3,2,1,0:T(8,128)} %copy.10, f32[2,2,384,256]{3,2,1,0:T(8,128)S(1)} %constant_dynamic-update-slice_fusion, f32[2,2,384,64]{3,2,1,0:T(8,128)} %copy.9), kind=kLoop, calls=%fused_computation | loop fusion | flops 1179648 | bytes 4718592 | tf_op jit(solution)/shard_map/concatenate | solution.py:32
  33.9 29.9 %shard_map.68 = (f32[2,2,384,384]{3,2,1,0:T(8,128)}, f32[3,2,256,256]{3,2,1,0:T(8,128)}) custom-call(s32[1,1,2,2]{3,2,1,0:T(2,128)S(1)} %copy-done.4, f32[2,2,384,384]{3,2,1,0:T(8,128)} %pad_maximum_fusion.ext, f32[3,2,256,256]{3,2,1,0:T(8,128)S(1)} %copy-done, f32[1,1,2,256,256]{4,3,2,1,0:T(8,128)S(1)} %copy-done.3, bf16[6,2,256,256]{3,2,1,0:T(8,128)(2,1)S(1)} %copy-done.1), custom_call_target="tpu_custom_call" | custom-call | tf_op jit(solution)/shard_map/pallas_call | solution.py:196
  63.7 1.2 slice.47
  64.9 5.7 %collective-permute-start.4 = (f32[2,2,64,384]{3,2,1,0:T(8,128)S(1)}, f32[2,2,64,384]{3,2,1,0:T(8,128)S(1)}, u32[]{:S(2)}, u32[]{:S(2)}) collective-permute-start(f32[2,2,64,384]{3,2,1,0:T(8,128)S(1)} %slice.47), channel_id=1, source_target_pairs={{0,4},{4,8},{8,12},{1,5},{5,9},{9,13},{2,6},{6,10},{10,14},{3,7},{... | collective-permute-start | bytes 1179656 | tf_op jit(solution)/shard_map/ppermute | solution.py:20
  71.8 1.2 slice_add_fusion.3
  73.0 1.3 collective-permute-start.5
  74.3 5.4 %collective-permute-done.5 = f32[2,2,64,384]{3,2,1,0:T(8,128)S(1)} collective-permute-done((f32[2,2,64,384]{3,2,1,0:T(8,128)S(1)}, f32[2,2,64,384]{3,2,1,0:T(8,128)S(1)}, u32[]{:S(2)}, u32[]{:S(2)}) %collective-permute-start.5) | collective-permute-done | bytes 393248 | tf_op jit(solution)/shard_map/ppermute | solution.py:20
  81.0 5.2 %collective-permute-start.6 = (f32[2,2,256,64]{3,2,1,0:T(8,128)}, f32[2,2,256,64]{3,2,1,0:T(8,128)}, u32[]{:S(2)}, u32[]{:S(2)}) collective-permute-start(f32[2,2,256,64]{3,2,1,0:T(8,128)} %slice.59), channel_id=1, source_target_pairs={{0,1},{1,2},{2,3},{4,5},{5,6},{6,7},{8,9},{9,10},{10,11},{12,13},{... | collective-permute-start | bytes 786440 | tf_op jit(solution)/shard_map/ppermute | solution.py:20
  86.2 6.2 %collective-permute-done.6 = f32[2,2,256,64]{3,2,1,0:T(8,128)} collective-permute-done((f32[2,2,256,64]{3,2,1,0:T(8,128)}, f32[2,2,256,64]{3,2,1,0:T(8,128)}, u32[]{:S(2)}, u32[]{:S(2)}) %collective-permute-start.6) | collective-permute-done | bytes 262176 | tf_op jit(solution)/shard_map/ppermute | solution.py:20
  92.3 2.2 %slice_add_fusion.1 = (f32[2,2,256,64]{3,2,1,0:T(8,128)}, f32[2,2,256,64]{3,2,1,0:T(8,128)}) fusion(f32[2,2,256,64]{3,2,1,0:T(8,128)} %collective-permute-done.6, f32[2,2,256,384]{3,2,1,0:T(8,128)S(1)} %pad_maximum_fusion.1), kind=kLoop, calls=%fused_computation.4 | loop fusion | flops 65536 | bytes 1310720 | tf_op jit(solution)/shard_map/add | solution.py:230
  94.5 1.3 collective-permute-start.7
  96.6 91.5 %all-reduce.2.cloned.1.call-done.summed = f32[3,2,256,256]{3,2,1,0:T(8,128)} async-done(((f32[3,2,256,256]{3,2,1,0:T(8,128)}), f32[3,2,256,256]{3,2,1,0:T(8,128)}) %all-reduce.2.cloned.1.call-update) | async-done | bytes 1572880 | tf_op jit(solution)/shard_map/psum | solution.py:241
  188.2 1.4 copy-done.2
  189.6 2.5 %shard_map.69 = f32[3,2,256,256]{3,2,1,0:T(8,128)} custom-call(f32[3,2,256,256]{3,2,1,0:T(8,128)S(1)} %copy-done, f32[3,2,256,256]{3,2,1,0:T(8,128)S(1)} %copy-done.2), custom_call_target="tpu_custom_call" | custom-call | tf_op jit(solution)/shard_map/pallas_call | solution.py:216
  192.1 1.2 slice_add_fusion
  193.5 1.4 pad_maximum_fusion.2
  (35 shorter events, 6.3 us)
Async XLA Ops:
  7.2 4.9 %copy-start.6 = (f32[2,2,256,256]{3,2,1,0:T(8,128)S(1)}, f32[2,2,256,256]{3,2,1,0:T(8,128)}, u32[]{:S(2)}) copy-start(f32[2,2,256,256]{3,2,1,0:T(8,128)} %param.5) | copy-start | bytes 3145732
  7.2 181.0 %all-reduce.2.cloned.1.call-start = ((), (), s32[]{:S(2)}) async-start(), calls=%async_computation | async-start | bytes 3145728 | tf_op jit(solution)/shard_map/psum | solution.py:241
  8.4 3.7 %collective-permute-start = (f32[2,2,64,256]{3,2,1,0:T(8,128)S(1)}, f32[2,2,64,256]{3,2,1,0:T(8,128)S(1)}, u32[]{:S(2)}, u32[]{:S(2)}) collective-permute-start(f32[2,2,64,256]{3,2,1,0:T(8,128)S(1)} %get-tuple-element.13), channel_id=1, source_target_pairs={{0,4},{4,8},{8,12},{1,5},{5,9},{9,13},{2,6},{6,10},{10,14},{3,7},{... | collective-permute-start | bytes 786440 | tf_op jit(solution)/shard_map/ppermute | solution.py:28
  10.8 5.5 %collective-permute-start.1 = (f32[2,2,64,256]{3,2,1,0:T(8,128)S(1)}, f32[2,2,64,256]{3,2,1,0:T(8,128)S(1)}, u32[]{:S(2)}, u32[]{:S(2)}) collective-permute-start(f32[2,2,64,256]{3,2,1,0:T(8,128)S(1)} %get-tuple-element.12), channel_id=1, source_target_pairs={{4,0},{8,4},{12,8},{5,1},{9,5},{13,9},{6,2},{10,6},{14,10},{7,3},{... | collective-permute-start | bytes 786440 | tf_op jit(solution)/shard_map/ppermute | solution.py:31
  16.8 10.0 %collective-permute-start.3 = (f32[2,2,384,64]{2,3,1,0:T(8,128)S(1)}, f32[2,2,384,64]{2,3,1,0:T(8,128)S(1)}, u32[]{:S(2)}, u32[]{:S(2)}) collective-permute-start(f32[2,2,384,64]{2,3,1,0:T(8,128)S(1)} %copy.8), channel_id=1, source_target_pairs={{1,0},{2,1},{3,2},{5,4},{6,5},{7,6},{9,8},{10,9},{11,10},{13,12},{... | collective-permute-start | bytes 1179656 | tf_op jit(solution)/shard_map/ppermute | solution.py:31
  18.4 10.5 %collective-permute-start.2 = (f32[2,2,384,64]{2,3,1,0:T(8,128)S(1)}, f32[2,2,384,64]{2,3,1,0:T(8,128)S(1)}, u32[]{:S(2)}, u32[]{:S(2)}) collective-permute-start(f32[2,2,384,64]{2,3,1,0:T(8,128)S(1)} %copy.7), channel_id=1, source_target_pairs={{0,1},{1,2},{2,3},{4,5},{5,6},{6,7},{8,9},{9,10},{10,11},{12,13},{... | collective-permute-start | bytes 1179656 | tf_op jit(solution)/shard_map/ppermute | solution.py:28
  30.0 3.9 %copy-start = (f32[3,2,256,256]{3,2,1,0:T(8,128)S(1)}, f32[3,2,256,256]{3,2,1,0:T(8,128)}, u32[]{:S(2)}) copy-start(f32[3,2,256,256]{3,2,1,0:T(8,128)} %probe.3) | copy-start | bytes 4718596
  30.0 3.9 %copy-start.1 = (bf16[6,2,256,256]{3,2,1,0:T(8,128)(2,1)S(1)}, bf16[6,2,256,256]{3,2,1,0:T(8,128)(2,1)}, u32[]{:S(2)}) copy-start(bf16[6,2,256,256]{3,2,1,0:T(8,128)(2,1)} %constant.2.clone.tab) | copy-start | bytes 4718596
  30.0 3.9 %copy-start.3 = (f32[1,1,2,256,256]{4,3,2,1,0:T(8,128)S(1)}, f32[1,1,2,256,256]{4,3,2,1,0:T(8,128)}, u32[]{:S(2)}) copy-start(f32[1,1,2,256,256]{4,3,2,1,0:T(8,128)} %meas.1) | copy-start | bytes 1572868
  30.0 3.9 %copy-start.4 = (s32[1,1,2,2]{3,2,1,0:T(2,128)S(1)}, s32[1,1,2,2]{3,2,1,0:T(2,128)}, u32[]{:S(2)}) copy-start(s32[1,1,2,2]{3,2,1,0:T(2,128)} %offs.1) | copy-start | bytes 52
  63.7 10.5 %copy-start.5 = (f32[2,2,384,384]{3,2,1,0:T(8,128)S(1)}, f32[2,2,384,384]{3,2,1,0:T(8,128)}, u32[]{:S(2)}) copy-start(f32[2,2,384,384]{3,2,1,0:T(8,128)} %get-tuple-element.4) | copy-start | bytes 7077892
  64.9 6.9 %collective-permute-start.4 = (f32[2,2,64,384]{3,2,1,0:T(8,128)S(1)}, f32[2,2,64,384]{3,2,1,0:T(8,128)S(1)}, u32[]{:S(2)}, u32[]{:S(2)}) collective-permute-start(f32[2,2,64,384]{3,2,1,0:T(8,128)S(1)} %slice.47), channel_id=1, source_target_pairs={{0,4},{4,8},{8,12},{1,5},{5,9},{9,13},{2,6},{6,10},{10,14},{3,7},{... | collective-permute-start | bytes 1179656 | tf_op jit(solution)/shard_map/ppermute | solution.py:20
  73.0 6.8 %collective-permute-start.5 = (f32[2,2,64,384]{3,2,1,0:T(8,128)S(1)}, f32[2,2,64,384]{3,2,1,0:T(8,128)S(1)}, u32[]{:S(2)}, u32[]{:S(2)}) collective-permute-start(f32[2,2,64,384]{3,2,1,0:T(8,128)S(1)} %get-tuple-element.7), channel_id=1, source_target_pairs={{4,0},{8,4},{12,8},{5,1},{9,5},{13,9},{6,2},{10,6},{14,10},{7,3},{... | collective-permute-start | bytes 1179656 | tf_op jit(solution)/shard_map/ppermute | solution.py:20
  81.0 11.4 %collective-permute-start.6 = (f32[2,2,256,64]{3,2,1,0:T(8,128)}, f32[2,2,256,64]{3,2,1,0:T(8,128)}, u32[]{:S(2)}, u32[]{:S(2)}) collective-permute-start(f32[2,2,256,64]{3,2,1,0:T(8,128)} %slice.59), channel_id=1, source_target_pairs={{0,1},{1,2},{2,3},{4,5},{5,6},{6,7},{8,9},{9,10},{10,11},{12,13},{... | collective-permute-start | bytes 786440 | tf_op jit(solution)/shard_map/ppermute | solution.py:20
  94.5 97.6 %collective-permute-start.7 = (f32[2,2,256,64]{3,2,1,0:T(8,128)}, f32[2,2,256,64]{3,2,1,0:T(8,128)}, u32[]{:S(2)}, u32[]{:S(2)}) collective-permute-start(f32[2,2,256,64]{3,2,1,0:T(8,128)} %get-tuple-element.9), channel_id=1, source_target_pairs={{1,0},{2,1},{3,2},{5,4},{6,5},{7,6},{9,8},{10,9},{11,10},{13,12},{... | collective-permute-start | bytes 786440 | tf_op jit(solution)/shard_map/ppermute | solution.py:20
  188.2 1.4 copy-start.2
  192.1 1.2 copy-start.7
  192.1 1.4 copy-start.8
Sparse Core Ops, SparseCore 0:
  86.3 101.8 all-reduce.1
where the time goes:
time: 202 us
  waiting for transfers between devices  113 us (56%)
  Pallas kernels  32.4 us (16%)
  starting transfers between devices  23 us (11%)
  between operations  14.2 us (7%)
  other arithmetic  9.99 us (5%)
  local copies, waits for them, and re-layouts  8.98 us (4%)
    psum x1, waiting for transfers between devices, shards(): summed = lax.psum(local_grad, ('row', 'col'))  91.5 us
    pallas_call x1, Pallas kernels, gradients(): pl.pallas_call(gradient_kernel, out_shape=(jax.ShapeDtypeStruct(extended....  29.9 us
    ppermute x4, starting transfers between devices, shifted(): return lax.ppermute(block, axis, route)  13.5 us
    ppermute x4, waiting for transfers between devices, shifted(): return lax.ppermute(block, axis, route)  12.8 us
    ppermute x2, waiting for transfers between devices, with_halo(): lax.ppermute(lax.slice_in_dim(block, 0, width, axis=dim), axis, backward)  7.98 us
    ppermute x2, starting transfers between devices, with_halo(): lax.ppermute(lax.slice_in_dim(block, block.shape[dim] - width, None, axis...  6.94 us
  transfers between devices with their start and end apart: 9, of which 7 were waited for; matrix products, arithmetic and copies ran while one was open for 2% of the time, Pallas kernels for 1%

commit v1 on v0

--- a/solution.py
+++ b/solution.py
@@ -12,12 +12,6 @@
 HALO = 64
 EPSILON = 1e-06
 PROP_PHASE = 40.0
-
-
-def shifted(block, axis, distance):
-    devices = range(lax.axis_size(axis))
-    route = [(i - distance, i) for i in devices if i - distance in devices]
-    return lax.ppermute(block, axis, route)
 
 
 def with_halo(block, sides, width):
@@ -212,35 +206,258 @@
     )(offsets, extended, probe_modes, measured, tables)
 
 
-def new_modes(probe_modes, summed):
+def halves(top, bottom, lane):
+    return jnp.where(lane < HALO, top, bottom)
+
+
+def exchange_kernel(nx, nc, ext, pgrad, summed, row_bands, col_bands, packed, buf_core, acc_core,
+                    buf_x, acc_x, buf_col, send, recv, fold_send, fold_recv):
+    modes, _, size, _ = pgrad.shape
+    layers, wide = ext.shape[0], ext.shape[3]
+    row, col = lax.axis_index("row"), lax.axis_index("col")
+    core, x = lax.rem(row, 2), row // 2
+    mate = row + 1 - 2 * core
+    other = row - 1 + 2 * core
+    rows_total = 2 * nx
+    has_other = (other >= 0) & (other < rows_total)
+    x_peers = [lax.rem(x + d, nx) for d in range(1, nx)]
+    col_peers = [lax.rem(col + d, nc) for d in range(1, nc)]
+    kind = pl.DeviceIdType.MESH
+
+    barrier = pltpu.get_barrier_semaphore()
+    targets = [{"row": mate}]
+    targets += [{"row": 2 * peer + core} for peer in x_peers]
+    targets += [{"col": peer} for peer in col_peers]
+    for target in targets:
+        pl.semaphore_signal(barrier, inc=1, device_id=target, device_id_type=kind)
+
+    @pl.when(has_other)
+    def _():
+        pl.semaphore_signal(barrier, inc=1, device_id={"row": other}, device_id_type=kind)
+        pl.semaphore_wait(barrier, len(targets) + 1)
+
+    @pl.when(jnp.logical_not(has_other))
+    def _():
+        pl.semaphore_wait(barrier, len(targets))
+
+    def remote(src, dst, sems, target):
+        return pltpu.make_async_remote_copy(
+            src_ref=src, dst_ref=dst, send_sem=sems[0], recv_sem=sems[1],
+            device_id=target, device_id_type=kind,
+        )
+
+    def sems(m, stage, d):
+        return send.at[m, stage, d], recv.at[m, stage, d]
+
+    n = size // nx
+    h = 2 * n // nc
+
+    def piece(k):
+        return pl.ds(pl.multiple_of((k // 2) * h, h), h), pl.ds(
+            pl.multiple_of(lax.rem(k, 2) * 128, 128), 128
+        )
+
+    def strip(k):
+        return pl.ds(pl.multiple_of(k * n, n), n)
+
+    my_rows, my_lanes = piece(col)
+    own_rows = pl.ds(pl.multiple_of(x * n + (col // 2) * h, h), h)
+
+    def stage(m, s):
+        if s == 0:
+            return [remote(pgrad.at[m, 1 - core], buf_core.at[m], sems(m, s, 0), {"row": mate})]
+        if s == 1:
+            return [
+                remote(acc_core.at[m, strip(peer)], buf_x.at[m, d], sems(m, s, d),
+                       {"row": 2 * peer + core})
+                for d, peer in enumerate(x_peers)
+            ]
+        if s == 2:
+            return [
+                remote(acc_x.at[m, piece(peer)[0], piece(peer)[1]], buf_col.at[m, d],
+                       sems(m, s, d), {"col": peer})
+                for d, peer in enumerate(col_peers)
+            ]
+        if s == 3:
+            ref = summed.at[m, core, own_rows, my_lanes]
+            return [remote(ref, ref, sems(m, s, d), {"col": peer})
+                    for d, peer in enumerate(col_peers)]
+        if s == 4:
+            ref = summed.at[m, core, strip(x)]
+            return [remote(ref, ref, sems(m, s, d), {"row": 2 * peer + core})
+                    for d, peer in enumerate(x_peers)]
+        ref = summed.at[m, core]
+        return [remote(ref, ref, sems(m, s, 0), {"row": mate})]
+
+    def finish(m, s):
+        for copy in copies[m, s]:
+            copy.wait_recv()
+        if s == 0:
+            acc_core[m] = pgrad[m, core] + buf_core[m]
+        if s == 1:
+            value = acc_core[m, strip(x)]
+            for d in range(nx - 1):
+                value = value + buf_x[m, d]
+            acc_x[m] = value
+        if s == 2:
+            value = acc_x[m, my_rows, my_lanes]
+            for d in range(nc - 1):
+                value = value + buf_col[m, d]
+            summed[m, core, own_rows, my_lanes] = value
+
+    copies = {}
+
+    def begin(m, s):
+        copies[m, s] = stage(m, s)
+        for copy in copies[m, s]:
+            copy.start()
+
+    def band(k, axis, at, limit, src, dst):
+        inside = (at >= 0) & (at < limit)
+        copy = remote(src, dst, (fold_send.at[k], fold_recv.at[k]), {axis: at})
+        return inside, copy
+
+    to_high = band(0, "row", row + 1, rows_total,
+                   ext.at[:, :, pl.ds(wide - HALO, HALO), :], row_bands.at[0])
+    to_low = band(1, "row", row - 1, rows_total, ext.at[:, :, pl.ds(0, HALO), :], row_bands.at[1])
+    right = band(2, "col", col + 1, nc, packed.at[0], col_bands.at[0])
+    left = band(3, "col", col - 1, nc, packed.at[1], col_bands.at[1])
+
+    def start(pair):
+        pl.when(pair[0])(pair[1].start)
+
+    def arrive(pair, inside, ref):
+        pl.when(inside)(pair[1].wait_recv)
+
+        @pl.when(jnp.logical_not(inside))
+        def _():
+            ref[...] = jnp.zeros_like(ref)
+
+    for m in range(modes):
+        begin(m, 0)
+    start(to_high)
+    start(to_low)
+    for m in range(modes):
+        finish(m, 0)
+        begin(m, 1)
+    arrive(to_high, row > 0, row_bands.at[0])
+    arrive(to_low, row < rows_total - 1, row_bands.at[1])
+    lane = lax.broadcasted_iota(jnp.int32, (size // 2, 128), 1)
+    for l in range(layers):
+        for c in range(2):
+            for slot, at in ((0, wide - 128), (1, 0)):
+                cut = pl.ds(at, 128)
+                half = size // 2
+                top = jnp.concatenate([
+                    ext[l, c, pl.ds(HALO, HALO), cut] + row_bands[0, l, c, :, cut],
+                    ext[l, c, pl.ds(2 * HALO, half - HALO), cut],
+                ], axis=0)
+                bottom = jnp.concatenate([
+                    ext[l, c, pl.ds(HALO + half, half - HALO), cut],
+                    ext[l, c, pl.ds(size, HALO), cut] + row_bands[1, l, c, :, cut],
+                ], axis=0)
+                if slot == 0:
+                    top = pltpu.roll(top, HALO, 1)
+                else:
+                    bottom = pltpu.roll(bottom, HALO, 1)
+                packed[slot, l, c] = halves(top, bottom, lane)
+    start(right)
+    start(left)
+    for wave in range(modes + 4):
+        for m in range(modes):
+            s = 1 + wave - m
+            if 1 <= s <= 4:
+                finish(m, s)
+                begin(m, s + 1)
+    for m in range(modes):
+        finish(m, 5)
+    arrive(right, col > 0, col_bands.at[0])
+    arrive(left, col < nc - 1, col_bands.at[1])
+    for group in copies.values():
+        for copy in group:
+            copy.wait_send()
+    for pair in (to_high, to_low, right, left):
+        pl.when(pair[0])(pair[1].wait_send)
+
+
+def exchange(grad_ext, local_grad):
+    modes, _, size, _ = local_grad.shape
+    layers, wide = grad_ext.shape[0], grad_ext.shape[3]
+    nx, nc = lax.axis_size("row") // 2, lax.axis_size("col")
+    n = size // nx
+    h = 2 * n // nc
+    f32 = jnp.float32
+    vmem = pl.BlockSpec(memory_space=pltpu.VMEM)
+    most = max(nx, nc) - 1
+    dma = pltpu.SemaphoreType.DMA
     return pl.pallas_call(
-        update_modes,
-        out_shape=jax.ShapeDtypeStruct(probe_modes.shape, jnp.float32),
-        compiler_params=pltpu.CompilerParams(vmem_limit_bytes=32 << 20),
-    )(probe_modes, summed)
-
-
-def fold(edge_grad, axis, dim):
-    count = edge_grad.shape[dim]
-    cut = functools.partial(lax.slice_in_dim, edge_grad, axis=dim)
-    from_high = shifted(cut(0, HALO), axis, -1)
-    from_low = shifted(cut(count - HALO, count), axis, 1)
-    return jnp.concatenate(
-        [
-            cut(HALO, 2 * HALO) + from_low,
-            cut(2 * HALO, count - 2 * HALO),
-            cut(count - 2 * HALO, count - HALO) + from_high,
+        functools.partial(exchange_kernel, nx, nc),
+        out_shape=(
+            jax.ShapeDtypeStruct(local_grad.shape, f32),
+            jax.ShapeDtypeStruct((2, layers, 2, HALO, wide), f32),
+            jax.ShapeDtypeStruct((2, layers, 2, size // 2, 128), f32),
+        ),
+        in_specs=[vmem, vmem],
+        out_specs=(vmem, vmem, vmem),
+        scratch_shapes=[
+            pltpu.VMEM((2, layers, 2, size // 2, 128), f32),
+            pltpu.VMEM((modes, size, size), f32),
+            pltpu.VMEM((modes, size, size), f32),
+            pltpu.VMEM((modes, nx - 1, n, size), f32),
+            pltpu.VMEM((modes, n, size), f32),
+            pltpu.VMEM((modes, nc - 1, h, 128), f32),
+            dma((modes, 6, most)),
+            dma((modes, 6, most)),
+            dma((4,)),
+            dma((4,)),
         ],
-        axis=dim,
-    )
+        compiler_params=pltpu.CompilerParams(
+            collective_id=0, has_side_effects=True, vmem_limit_bytes=48 << 20
+        ),
+    )(grad_ext, local_grad)
+
+
+def last_kernel(ext, row_bands, col_bands, probe, summed, grad, out):
+    layers, wide = ext.shape[0], ext.shape[3]
+    size = grad.shape[3]
+    half = size // 2
+    lane = lax.broadcasted_iota(jnp.int32, (half, 128), 1)
+    for l in range(layers):
+        for c in range(2):
+            full = jnp.concatenate([
+                ext[l, c, pl.ds(HALO, HALO), :] + row_bands[0, l, c],
+                ext[l, c, pl.ds(2 * HALO, size - 2 * HALO), :],
+                ext[l, c, pl.ds(size, HALO), :] + row_bands[1, l, c],
+            ], axis=0)
+            full = pltpu.roll(full, wide - HALO, 1)[:, :size]
+            low, high = col_bands[0, l, c], col_bands[1, l, c]
+            low_turned, high_turned = pltpu.roll(low, HALO, 1), pltpu.roll(high, HALO, 1)
+            for at, low_part, high_part in ((0, low, high_turned), (half, low_turned, high)):
+                rows = full[at:at + half]
+                grad[l, c, pl.ds(at, half), pl.ds(0, 128)] = rows[:, :128] + halves(
+                    low_part, 0.0, lane)
+                grad[l, c, pl.ds(at, half), pl.ds(size - 128, 128)] = rows[:, 128:] + halves(
+                    0.0, high_part, lane)
+    update_modes(probe, summed, out)
+
+
+def last(grad_ext, row_bands, col_bands, probe_modes, summed, grad_shape):
+    f32 = jnp.float32
+    return pl.pallas_call(
+        last_kernel,
+        out_shape=(
+            jax.ShapeDtypeStruct(grad_shape, f32),
+            jax.ShapeDtypeStruct(probe_modes.shape, f32),
+        ),
+        compiler_params=pltpu.CompilerParams(vmem_limit_bytes=40 << 20),
+    )(grad_ext, row_bands, col_bands, probe_modes, summed)
 
 
 def shards(object_field, probe_modes, measured, offsets):
     extended = with_halo(object_field, (("row", 2), ("col", 3)), HALO)
     grad_ext, local_grad = gradients(offsets, extended, probe_modes, measured)
-    summed = lax.psum(local_grad, ("row", "col"))
-    object_grad = fold(fold(grad_ext, "row", 2), "col", 3)
-    return (object_grad, new_modes(probe_modes, summed))
+    summed, row_bands, col_bands = exchange(grad_ext, local_grad)
+    return last(grad_ext, row_bands, col_bands, probe_modes, summed, object_field.shape)
 
 
 def solution(mesh):

time: 202 us -> 109 us (0.54)
  waiting for transfers between devices: 113 us -> 8.99 us
  Pallas kernels: 32.4 us -> 82.4 us
  between operations: 14.2 us -> 0.78 us
  starting transfers between devices: 23 us -> 10.3 us
  other arithmetic: 9.99 us -> 2.3 us
  local copies, waits for them, and re-layouts: 8.98 us -> 3.63 us
    psum x1 -> x0, waiting for transfers between devices: 91.5 us -> none  [shards(): summed = lax.psum(local_grad, ('row', 'col'))]
    pallas_call x1 -> x2, Pallas kernels: 2.54 us -> 52.3 us  [the longest x1 48.9 us: exchange(): pl.pallas_call(functools.partial(exchange_kernel, nx, nc), out_shape=(jax...]
    ppermute x4 -> x0, starting transfers between devices: 13.5 us -> none  [shifted(): return lax.ppermute(block, axis, route)]
    ppermute x4 -> x0, waiting for transfers between devices: 12.8 us -> none  [shifted(): return lax.ppermute(block, axis, route)]
    add x4 -> x0, other arithmetic: 4.59 us -> none  [the longest x2 3.35 us: fold(): cut(HALO, 2 * HALO) + from_low]
    slice x4 -> x0, local copies, waits for them, and re-layouts: 3.06 us -> none  [the longest x2 2.17 us: fold(): from_low = shifted(cut(count - HALO, count), axis, 1)]
  transfers between devices with their start and end apart: 9 -> 4, of which waited for: 7 -> 3; matrix products, arithmetic and copies ran while one was open for 2% -> 1% of each run, Pallas kernels for 1% -> 0%
where the time goes in v1:
time: 109 us; the launch traced here: 108 us
  Pallas kernels  82.4 us (76%)
  starting transfers between devices  10.3 us (9%)
  waiting for transfers between devices  8.99 us (8%)
  local copies, waits for them, and re-layouts  3.63 us (3%)
  other arithmetic  2.3 us (2%)
    pallas_call x1, Pallas kernels, exchange(): pl.pallas_call(functools.partial(exchange_kernel, nx, nc), out_shape=(jax...  48.9 us
    pallas_call x1, Pallas kernels, gradients(): pl.pallas_call(gradient_kernel, out_shape=(jax.ShapeDtypeStruct(extended....  30.1 us
    ppermute x2, starting transfers between devices, with_halo(): lax.ppermute(lax.slice_in_dim(block, block.shape[dim] - width, None, axis...  7.67 us
    ppermute x2, waiting for transfers between devices, with_halo(): lax.ppermute(lax.slice_in_dim(block, 0, width, axis=dim), axis, backward)  7.26 us
    pallas_call x1, Pallas kernels, last(): pl.pallas_call(last_kernel, out_shape=(jax.ShapeDtypeStruct(grad_shape, f...  3.36 us
    ppermute x2, starting transfers between devices, with_halo(): lax.ppermute(lax.slice_in_dim(block, 0, width, axis=dim), axis, backward)  2.58 us
    concatenate x1, other arithmetic, with_halo(): block = jnp.concatenate([low, block, high], axis=dim)  2.3 us
  transfers between devices with their start and end apart: 4, of which 3 were waited for; matrix products, arithmetic and copies ran while one was open for 1% of the time, Pallas kernels for 0%

profile of v1, /device:TPU:0, one launch (start us, length us, event | category | flops | bytes accessed | tf_op | source)
XLA Modules:
  0.0 108.3 jit_solution(8879441881369256445)
XLA Ops:
  0.6 1.2 %fusion.1 = (f32[2,2,64,256]{3,2,1,0:T(8,128)S(1)}, f32[2,2,64,256]{3,2,1,0:T(8,128)S(1)}) fusion(f32[2,2,256,256]{3,2,1,0:T(8,128)} %param.5), kind=kLoop, calls=%fused_computation.5 | loop fusion | bytes 1048576 | tf_op jit(solution)/shard_map/slice | solution.py:25
  1.8 2.4 %collective-permute-start = (f32[2,2,64,256]{3,2,1,0:T(8,128)S(1)}, f32[2,2,64,256]{3,2,1,0:T(8,128)S(1)}, u32[]{:S(2)}, u32[]{:S(2)}) collective-permute-start(f32[2,2,64,256]{3,2,1,0:T(8,128)S(1)} %get-tuple-element.15), channel_id=1, source_target_pairs={{0,4},{4,8},{8,12},{1,5},{5,9},{9,13},{2,6},{6,10},{10,14},{3,7},{... | collective-permute-start | bytes 786440 | tf_op jit(solution)/shard_map/ppermute | solution.py:22
  4.2 1.3 %collective-permute-start.1 = (f32[2,2,64,256]{3,2,1,0:T(8,128)S(1)}, f32[2,2,64,256]{3,2,1,0:T(8,128)S(1)}, u32[]{:S(2)}, u32[]{:S(2)}) collective-permute-start(f32[2,2,64,256]{3,2,1,0:T(8,128)S(1)} %get-tuple-element.14), channel_id=1, source_target_pairs={{4,0},{8,4},{12,8},{5,1},{9,5},{13,9},{6,2},{10,6},{14,10},{7,3},{... | collective-permute-start | bytes 786440 | tf_op jit(solution)/shard_map/ppermute | solution.py:25
  5.5 0.0 collective-permute-done
  5.5 0.1 constant_dynamic-update-slice_fusion.1
  5.6 4.1 %collective-permute-done.1 = f32[2,2,64,256]{3,2,1,0:T(8,128)S(1)} collective-permute-done((f32[2,2,64,256]{3,2,1,0:T(8,128)S(1)}, f32[2,2,64,256]{3,2,1,0:T(8,128)S(1)}, u32[]{:S(2)}, u32[]{:S(2)}) %collective-permute-start.1) | collective-permute-done | bytes 262176 | tf_op jit(solution)/shard_map/ppermute | solution.py:25
  9.7 0.3 fusion
  10.0 0.3 copy.8
  10.3 1.3 %collective-permute-start.3 = (f32[2,2,384,64]{2,3,1,0:T(8,128)S(1)}, f32[2,2,384,64]{2,3,1,0:T(8,128)S(1)}, u32[]{:S(2)}, u32[]{:S(2)}) collective-permute-start(f32[2,2,384,64]{2,3,1,0:T(8,128)S(1)} %copy.8), channel_id=1, source_target_pairs={{1,0},{2,1},{3,2},{5,4},{6,5},{7,6},{9,8},{10,9},{11,10},{13,12},{... | collective-permute-start | bytes 1179656 | tf_op jit(solution)/shard_map/ppermute | solution.py:25
  11.6 0.2 copy.7
  11.8 5.3 %collective-permute-start.2 = (f32[2,2,384,64]{2,3,1,0:T(8,128)S(1)}, f32[2,2,384,64]{2,3,1,0:T(8,128)}, u32[]{:S(2)}, u32[]{:S(2)}) collective-permute-start(f32[2,2,384,64]{2,3,1,0:T(8,128)S(1)} %copy.7), channel_id=1, source_target_pairs={{0,1},{1,2},{2,3},{4,5},{5,6},{6,7},{8,9},{9,10},{10,11},{12,13},{... | collective-permute-start | bytes 1179656 | tf_op jit(solution)/shard_map/ppermute | solution.py:22
  17.1 3.2 %collective-permute-done.3 = f32[2,2,384,64]{2,3,1,0:T(8,128)S(1)} collective-permute-done((f32[2,2,384,64]{2,3,1,0:T(8,128)S(1)}, f32[2,2,384,64]{2,3,1,0:T(8,128)S(1)}, u32[]{:S(2)}, u32[]{:S(2)}) %collective-permute-start.3) | collective-permute-done | bytes 393248 | tf_op jit(solution)/shard_map/ppermute | solution.py:25
  20.3 0.3 copy.10
  20.5 1.7 %collective-permute-done.2 = f32[2,2,384,64]{2,3,1,0:T(8,128)} collective-permute-done((f32[2,2,384,64]{2,3,1,0:T(8,128)S(1)}, f32[2,2,384,64]{2,3,1,0:T(8,128)}, u32[]{:S(2)}, u32[]{:S(2)}) %collective-permute-start.2) | collective-permute-done | bytes 393248 | tf_op jit(solution)/shard_map/ppermute | solution.py:22
  22.3 1.3 %copy.9 = f32[2,2,384,64]{3,2,1,0:T(8,128)S(1)} copy(f32[2,2,384,64]{2,3,1,0:T(8,128)} %collective-permute-done.2) | data formatting | bytes 786432 | tf_op jit(solution)/shard_map/ppermute | solution.py:22
  23.5 0.0 copy-start.1
  23.6 0.0 copy-start.2
  23.6 0.0 copy-start.3
  23.6 0.0 copy-start.4
  23.6 2.3 %pad_maximum_fusion.ext = f32[2,2,384,384]{3,2,1,0:T(8,128)} fusion(f32[2,2,384,64]{3,2,1,0:T(8,128)S(1)} %copy.10, f32[2,2,384,256]{3,2,1,0:T(8,128)S(1)} %constant_dynamic-update-slice_fusion, f32[2,2,384,64]{3,2,1,0:T(8,128)S(1)} %copy.9), kind=kLoop, calls=%fused_computation | loop fusion | flops 1179648 | bytes 4718592 | tf_op jit(solution)/shard_map/concatenate | solution.py:26
  25.9 0.0 copy-done.3
  25.9 30.1 %shard_map.68 = (f32[2,2,384,384]{3,2,1,0:T(8,128)}, f32[3,2,256,256]{3,2,1,0:T(8,128)S(1)}) custom-call(s32[1,1,2,2]{3,2,1,0:T(2,128)S(1)} %copy-done.4, f32[2,2,384,384]{3,2,1,0:T(8,128)} %pad_maximum_fusion.ext, f32[3,2,256,256]{3,2,1,0:T(8,128)S(1)} %copy-done.1, f32[1,1,2,256,256]{4,3,2,1,0:T(8,128)S(1)} %copy-done.3, bf16[6,2,256,256]{3,2,1,0:T(8,128)(2,1)S(1)} %copy-done.2), custom_call_target="tpu_custom_call" | custom-call | tf_op jit(solution)/shard_map/pallas_call | solution.py:190
  56.0 48.9 %shard_map.69 = (f32[3,2,256,256]{3,2,1,0:T(8,128)S(1)}, f32[2,2,2,64,384]{4,3,2,1,0:T(8,128)S(1)}, f32[2,2,2,128,128]{4,3,2,1,0:T(8,128)S(1)}) custom-call(f32[2,2,384,384]{3,2,1,0:T(8,128)} %get-tuple-element.7.ext, f32[3,2,256,256]{3,2,1,0:T(8,128)S(1)} %get-tuple-element.8.pgrad), custom_call_target="tpu_custom_call" | custom-call | tf_op jit(solution)/shard_map/pallas_call | solution.py:393
  105.0 3.4 %shard_map.70 = (f32[2,2,256,256]{3,2,1,0:T(8,128)}, f32[3,2,256,256]{3,2,1,0:T(8,128)}) custom-call(f32[2,2,384,384]{3,2,1,0:T(8,128)S(1)} %copy-done, f32[2,2,2,64,384]{4,3,2,1,0:T(8,128)S(1)} %get-tuple-element.9.row_bands, f32[2,2,2,128,128]{4,3,2,1,0:T(8,128)S(1)} %get-tuple-element.10.col_bands, f32[3,2,256,256]{3,2,1,0:T(8,128)S(1)} %copy-done.1, ...), custom_call_target="tpu_custom_call" | custom-call | tf_op jit(solution)/shard_map/pallas_call | solution.py:446
  (9 shorter events, 0.1 us)
Async XLA Ops:
  0.6 4.9 %copy-start.5 = (f32[2,2,256,256]{3,2,1,0:T(8,128)S(1)}, f32[2,2,256,256]{3,2,1,0:T(8,128)}, u32[]{:S(2)}) copy-start(f32[2,2,256,256]{3,2,1,0:T(8,128)} %param.5) | copy-start | bytes 3145732
  1.8 3.7 %collective-permute-start = (f32[2,2,64,256]{3,2,1,0:T(8,128)S(1)}, f32[2,2,64,256]{3,2,1,0:T(8,128)S(1)}, u32[]{:S(2)}, u32[]{:S(2)}) collective-permute-start(f32[2,2,64,256]{3,2,1,0:T(8,128)S(1)} %get-tuple-element.15), channel_id=1, source_target_pairs={{0,4},{4,8},{8,12},{1,5},{5,9},{9,13},{2,6},{6,10},{10,14},{3,7},{... | collective-permute-start | bytes 786440 | tf_op jit(solution)/shard_map/ppermute | solution.py:22
  4.2 5.5 %collective-permute-start.1 = (f32[2,2,64,256]{3,2,1,0:T(8,128)S(1)}, f32[2,2,64,256]{3,2,1,0:T(8,128)S(1)}, u32[]{:S(2)}, u32[]{:S(2)}) collective-permute-start(f32[2,2,64,256]{3,2,1,0:T(8,128)S(1)} %get-tuple-element.14), channel_id=1, source_target_pairs={{4,0},{8,4},{12,8},{5,1},{9,5},{13,9},{6,2},{10,6},{14,10},{7,3},{... | collective-permute-start | bytes 786440 | tf_op jit(solution)/shard_map/ppermute | solution.py:25
  10.3 10.0 %collective-permute-start.3 = (f32[2,2,384,64]{2,3,1,0:T(8,128)S(1)}, f32[2,2,384,64]{2,3,1,0:T(8,128)S(1)}, u32[]{:S(2)}, u32[]{:S(2)}) collective-permute-start(f32[2,2,384,64]{2,3,1,0:T(8,128)S(1)} %copy.8), channel_id=1, source_target_pairs={{1,0},{2,1},{3,2},{5,4},{6,5},{7,6},{9,8},{10,9},{11,10},{13,12},{... | collective-permute-start | bytes 1179656 | tf_op jit(solution)/shard_map/ppermute | solution.py:25
  11.8 10.5 %collective-permute-start.2 = (f32[2,2,384,64]{2,3,1,0:T(8,128)S(1)}, f32[2,2,384,64]{2,3,1,0:T(8,128)}, u32[]{:S(2)}, u32[]{:S(2)}) collective-permute-start(f32[2,2,384,64]{2,3,1,0:T(8,128)S(1)} %copy.7), channel_id=1, source_target_pairs={{0,1},{1,2},{2,3},{4,5},{5,6},{6,7},{8,9},{9,10},{10,11},{12,13},{... | collective-permute-start | bytes 1179656 | tf_op jit(solution)/shard_map/ppermute | solution.py:22
  23.5 2.3 %copy-start.1 = (f32[3,2,256,256]{3,2,1,0:T(8,128)S(1)}, f32[3,2,256,256]{3,2,1,0:T(8,128)}, u32[]{:S(2)}) copy-start(f32[3,2,256,256]{3,2,1,0:T(8,128)} %probe.3) | copy-start | bytes 4718596
  23.6 2.3 %copy-start.2 = (bf16[6,2,256,256]{3,2,1,0:T(8,128)(2,1)S(1)}, bf16[6,2,256,256]{3,2,1,0:T(8,128)(2,1)}, u32[]{:S(2)}) copy-start(bf16[6,2,256,256]{3,2,1,0:T(8,128)(2,1)} %constant.2.clone.tab) | copy-start | bytes 4718596
  23.6 2.4 %copy-start.3 = (f32[1,1,2,256,256]{4,3,2,1,0:T(8,128)S(1)}, f32[1,1,2,256,256]{4,3,2,1,0:T(8,128)}, u32[]{:S(2)}) copy-start(f32[1,1,2,256,256]{4,3,2,1,0:T(8,128)} %meas.1) | copy-start | bytes 1572868
  23.6 2.4 %copy-start.4 = (s32[1,1,2,2]{3,2,1,0:T(2,128)S(1)}, s32[1,1,2,2]{3,2,1,0:T(2,128)}, u32[]{:S(2)}) copy-start(s32[1,1,2,2]{3,2,1,0:T(2,128)} %offs.1) | copy-start | bytes 52
  56.0 48.9 %copy-start = (f32[2,2,384,384]{3,2,1,0:T(8,128)S(1)}, f32[2,2,384,384]{3,2,1,0:T(8,128)}, u32[]{:S(2)}) copy-start(f32[2,2,384,384]{3,2,1,0:T(8,128)} %get-tuple-element.7.ext) | copy-start | bytes 7077892

commit v2 on v1

--- a/solution.py
+++ b/solution.py
@@ -12,19 +12,6 @@
 HALO = 64
 EPSILON = 1e-06
 PROP_PHASE = 40.0
-
-
-def with_halo(block, sides, width):
-    for axis, dim in sides:
-        count = lax.axis_size(axis)
-        forward = [(i, i + 1) for i in range(count - 1)]
-        backward = [(target, source) for source, target in forward]
-        low = lax.ppermute(
-            lax.slice_in_dim(block, block.shape[dim] - width, None, axis=dim), axis, forward
-        )
-        high = lax.ppermute(lax.slice_in_dim(block, 0, width, axis=dim), axis, backward)
-        block = jnp.concatenate([low, block, high], axis=dim)
-    return block
 
 
 def split_tables(size):
@@ -208,6 +195,136 @@
 
 def halves(top, bottom, lane):
     return jnp.where(lane < HALO, top, bottom)
+
+
+def halo_kernel(nr, nc, field, ext, packed, row_bands, corners, col_bands, col_corners, send, recv):
+    layers, _, size, _ = field.shape
+    half = size // 2
+    row, col = lax.axis_index("row"), lax.axis_index("col")
+    kind = pl.DeviceIdType.MESH
+    barrier = pltpu.get_barrier_semaphore()
+    for target in (
+        {"row": lax.rem(row + 1, nr)},
+        {"row": lax.rem(row + nr - 1, nr)},
+        {"col": lax.rem(col + 1, nc)},
+        {"col": lax.rem(col + nc - 1, nc)},
+    ):
+        pl.semaphore_signal(barrier, inc=1, device_id=target, device_id_type=kind)
+
+    planes = [(l, c) for l in range(layers) for c in range(2)]
+    lane = lax.broadcasted_iota(jnp.int32, (half, 128), 1)
+    edge = lax.broadcasted_iota(jnp.int32, (HALO, 128), 1)
+    for l, c in planes:
+        top, bottom = field[l, c, pl.ds(0, half)], field[l, c, pl.ds(half, half)]
+        packed[0, l, c] = halves(pltpu.roll(top[:, size - 128:], HALO, 1), bottom[:, size - 128:],
+                                 lane)
+        packed[1, l, c] = halves(top[:, :128], pltpu.roll(bottom[:, :128], HALO, 1), lane)
+    pl.semaphore_wait(barrier, 4)
+
+    def route(k, axis, at, limit, src, dst):
+        copy = pltpu.make_async_remote_copy(
+            src_ref=src, dst_ref=dst, send_sem=send.at[k], recv_sem=recv.at[k],
+            device_id={axis: at}, device_id_type=kind,
+        )
+        return (at >= 0) & (at < limit), copy
+
+    def start(pair):
+        pl.when(pair[0])(pair[1].start)
+
+    def arrive(pair, inside, ref):
+        pl.when(inside)(pair[1].wait_recv)
+
+        @pl.when(jnp.logical_not(inside))
+        def _():
+            ref[...] = jnp.zeros_like(ref)
+
+    to_high = route(0, "row", row + 1, nr, field.at[:, :, pl.ds(size - HALO, HALO)],
+                    row_bands.at[0])
+    to_low = route(1, "row", row - 1, nr, field.at[:, :, pl.ds(0, HALO)], row_bands.at[1])
+    right = route(2, "col", col + 1, nc, packed.at[0], col_bands.at[0])
+    left = route(3, "col", col - 1, nc, packed.at[1], col_bands.at[1])
+    right_corner = route(4, "col", col + 1, nc, corners.at[0], col_corners.at[0])
+    left_corner = route(5, "col", col - 1, nc, corners.at[1], col_corners.at[1])
+    start(to_high)
+    start(to_low)
+    start(right)
+    start(left)
+    arrive(to_high, row > 0, row_bands.at[0])
+    arrive(to_low, row < nr - 1, row_bands.at[1])
+    for l, c in planes:
+        low, high = row_bands[0, l, c], row_bands[1, l, c]
+        corners[0, l, c] = halves(pltpu.roll(low[:, size - 128:], HALO, 1), high[:, size - 128:],
+                                  edge)
+        corners[1, l, c] = halves(low[:, :128], pltpu.roll(high[:, :128], HALO, 1), edge)
+    start(right_corner)
+    start(left_corner)
+
+    def middle(l, c):
+        at = 0
+        for part in (row_bands[0, l, c], field[l, c], row_bands[1, l, c]):
+            tall = part.shape[0]
+            turned = [pltpu.roll(part[:, k:k + 128], HALO, 1) for k in range(0, size, 128)]
+            mask = lax.broadcasted_iota(jnp.int32, (tall, 128), 1)
+            spot = pl.ds(at, tall)
+            for k in range(len(turned) + 1):
+                before = turned[k - 1] if k else 0.0
+                after = turned[k] if k < len(turned) else 0.0
+                ext[l, c, spot, pl.ds(128 * k, 128)] = halves(before, after, mask)
+            at += tall
+
+    for l, c in planes:
+        middle(l, c)
+    wide = ext.shape[3]
+    first, final = pl.ds(0, 128), pl.ds(wide - 128, 128)
+
+    def sides(low_side, high_side, l, c, at, tall, mask):
+        low, high = low_side[l, c], high_side[l, c]
+        low_turned, high_turned = pltpu.roll(low, HALO, 1), pltpu.roll(high, HALO, 1)
+        for spot, low_part, high_part in (
+            (pl.ds(at[0], tall), low, high_turned),
+            (pl.ds(at[1], tall), low_turned, high),
+        ):
+            ext[l, c, spot, first] = halves(low_part, ext[l, c, spot, first], mask)
+            ext[l, c, spot, final] = halves(ext[l, c, spot, final], high_part, mask)
+
+    arrive(right, col > 0, col_bands.at[0])
+    arrive(left, col < nc - 1, col_bands.at[1])
+    for l, c in planes:
+        sides(col_bands.at[0], col_bands.at[1], l, c, (HALO, HALO + half), half, lane)
+    arrive(right_corner, col > 0, col_corners.at[0])
+    arrive(left_corner, col < nc - 1, col_corners.at[1])
+    for l, c in planes:
+        sides(col_corners.at[0], col_corners.at[1], l, c, (0, HALO + size), HALO, edge)
+    for pair in (to_high, to_low, right, left, right_corner, left_corner):
+        pl.when(pair[0])(pair[1].wait_send)
+
+
+def with_halo(field):
+    layers, _, size, _ = field.shape
+    wide = size + 2 * HALO
+    f32 = jnp.float32
+    vmem = pl.BlockSpec(memory_space=pltpu.VMEM)
+    dma = pltpu.SemaphoreType.DMA
+    side = pltpu.VMEM((2, layers, 2, size // 2, 128), f32)
+    corner = pltpu.VMEM((2, layers, 2, HALO, 128), f32)
+    return pl.pallas_call(
+        functools.partial(halo_kernel, lax.axis_size("row"), lax.axis_size("col")),
+        out_shape=jax.ShapeDtypeStruct((layers, 2, wide, wide), f32),
+        in_specs=[vmem],
+        out_specs=vmem,
+        scratch_shapes=[
+            side,
+            pltpu.VMEM((2, layers, 2, HALO, size), f32),
+            corner,
+            side,
+            corner,
+            dma((6,)),
+            dma((6,)),
+        ],
+        compiler_params=pltpu.CompilerParams(
+            collective_id=1, has_side_effects=True, vmem_limit_bytes=32 << 20
+        ),
+    )(field)
 
 
 def exchange_kernel(nx, nc, ext, pgrad, summed, row_bands, col_bands, packed, buf_core, acc_core,
@@ -454,7 +571,7 @@
 
 
 def shards(object_field, probe_modes, measured, offsets):
-    extended = with_halo(object_field, (("row", 2), ("col", 3)), HALO)
+    extended = with_halo(object_field)
     grad_ext, local_grad = gradients(offsets, extended, probe_modes, measured)
     summed, row_bands, col_bands = exchange(grad_ext, local_grad)
     return last(grad_ext, row_bands, col_bands, probe_modes, summed, object_field.shape)

time: 109 us -> 97.2 us (0.89)
  starting transfers between devices: 10.3 us -> 0 us
  Pallas kernels: 82.4 us -> 91.6 us
  waiting for transfers between devices: 8.99 us -> 0 us
  other arithmetic: 2.3 us -> 0 us
    pallas_call x0 -> x1, Pallas kernels: none -> 13.6 us  [with_halo(): pl.pallas_call(functools.partial(halo_kernel, lax.axis_size('row'), lax.a...]
    ppermute x4 -> x0, starting transfers between devices: 10.3 us -> none  [the longest x2 7.67 us: with_halo(): lax.ppermute(lax.slice_in_dim(block, block.shape[dim] - width, None, axis...]
    ppermute x4 -> x0, waiting for transfers between devices: 8.99 us -> none  [the longest x2 7.26 us: with_halo(): lax.ppermute(lax.slice_in_dim(block, 0, width, axis=dim), axis, backward)]
    pallas_call x1, Pallas kernels: 48.9 us -> 44.5 us  [exchange(): pl.pallas_call(functools.partial(exchange_kernel, nx, nc), out_shape=(jax...]
    unnamed x14, local copies, waits for them, and re-layouts: 0.17 us -> 3.83 us
    concatenate x1 -> x0, other arithmetic: 2.3 us -> none  [with_halo(): block = jnp.concatenate([low, block, high], axis=dim)]
    slice x4 -> x0, local copies, waits for them, and re-layouts: 1.92 us -> none  [the longest x2 1.41 us: with_halo(): lax.slice_in_dim(block, 0, width, axis=dim)]
    ppermute x2 -> x0, local copies, waits for them, and re-layouts: 1.52 us -> none  [the longest x1 1.26 us: with_halo(): lax.ppermute(lax.slice_in_dim(block, block.shape[dim] - width, None, axis...]
  transfers between devices with their start and end apart: 4 -> 0, of which waited for: 3 -> 0; matrix products, arithmetic and copies ran while one was open for 1% -> 0% of each run, Pallas kernels for 0% -> 0%
where the time goes in v2:
time: 97.2 us; the launch traced here: 96.1 us
  Pallas kernels  91.6 us (94%)
  local copies, waits for them, and re-layouts  3.83 us (4%)
    pallas_call x1, Pallas kernels, exchange(): pl.pallas_call(functools.partial(exchange_kernel, nx, nc), out_shape=(jax...  44.5 us
    pallas_call x1, Pallas kernels, gradients(): pl.pallas_call(gradient_kernel, out_shape=(jax.ShapeDtypeStruct(extended....  30.1 us
    pallas_call x1, Pallas kernels, with_halo(): pl.pallas_call(functools.partial(halo_kernel, lax.axis_size('row'), lax.a...  13.6 us
    unnamed x14, local copies, waits for them, and re-layouts  3.83 us
    pallas_call x1, Pallas kernels, last(): pl.pallas_call(last_kernel, out_shape=(jax.ShapeDtypeStruct(grad_shape, f...  3.36 us

profile of v2, /device:TPU:0, one launch (start us, length us, event | category | flops | bytes accessed | tf_op | source)
XLA Modules:
  0.0 96.1 jit_solution(18043697144156348675)
XLA Ops:
  0.6 0.0 copy-start.3
  0.6 0.0 copy-start.2
  0.7 0.0 copy-start.4
  0.7 1.4 %copy-done.4 = f32[2,2,256,256]{3,2,1,0:T(8,128)S(1)} copy-done((f32[2,2,256,256]{3,2,1,0:T(8,128)S(1)}, f32[2,2,256,256]{3,2,1,0:T(8,128)}, u32[]{:S(2)}) %copy-start.4) | copy-done | bytes 1048600
  2.0 0.0 copy-start.6
  2.0 13.6 %shard_map.68.ext = f32[2,2,384,384]{3,2,1,0:T(8,128)S(1)} custom-call(f32[2,2,256,256]{3,2,1,0:T(8,128)S(1)} %copy-done.4), custom_call_target="tpu_custom_call" | custom-call | tf_op jit(solution)/shard_map/pallas_call | solution.py:310
  15.7 0.0 copy-start
  15.7 1.4 %copy-done = f32[2,2,384,384]{3,2,1,0:T(8,128)} copy-done((f32[2,2,384,384]{3,2,1,0:T(8,128)}, f32[2,2,384,384]{3,2,1,0:T(8,128)S(1)}, u32[]{:S(2)}) %copy-start) | copy-done | bytes 2359320
  17.1 0.0 copy-done.3
  17.1 0.0 copy-done.2
  17.1 0.0 copy-done.6
  17.1 0.0 copy-start.5
  17.1 1.0 %copy-done.5 = f32[1,1,2,256,256]{4,3,2,1,0:T(8,128)S(1)} copy-done((f32[1,1,2,256,256]{4,3,2,1,0:T(8,128)S(1)}, f32[1,1,2,256,256]{4,3,2,1,0:T(8,128)}, u32[]{:S(2)}) %copy-start.5) | copy-done | bytes 524312
  18.1 30.1 %shard_map.69 = (f32[2,2,384,384]{3,2,1,0:T(8,128)}, f32[3,2,256,256]{3,2,1,0:T(8,128)S(1)}) custom-call(s32[1,1,2,2]{3,2,1,0:T(2,128)S(1)} %copy-done.6, f32[2,2,384,384]{3,2,1,0:T(8,128)} %copy-done, f32[3,2,256,256]{3,2,1,0:T(8,128)S(1)} %copy-done.2, f32[1,1,2,256,256]{4,3,2,1,0:T(8,128)S(1)} %copy-done.5, bf16[6,2,256,256]{3,2,1,0:T(8,128)(2,1)S(1)} %copy-done.3), custom_call_target="tpu_custom_call" | custom-call | tf_op jit(solution)/shard_map/pallas_call | solution.py:177
  48.3 0.0 copy-start.1
  48.3 44.5 %shard_map.70 = (f32[3,2,256,256]{3,2,1,0:T(8,128)S(1)}, f32[2,2,2,64,384]{4,3,2,1,0:T(8,128)S(1)}, f32[2,2,2,128,128]{4,3,2,1,0:T(8,128)S(1)}) custom-call(f32[2,2,384,384]{3,2,1,0:T(8,128)} %get-tuple-element.7.ext, f32[3,2,256,256]{3,2,1,0:T(8,128)S(1)} %get-tuple-element.8.pgrad), custom_call_target="tpu_custom_call" | custom-call | tf_op jit(solution)/shard_map/pallas_call | solution.py:510
  92.8 0.0 copy-done.1
  92.8 3.4 %shard_map.71 = (f32[2,2,256,256]{3,2,1,0:T(8,128)}, f32[3,2,256,256]{3,2,1,0:T(8,128)}) custom-call(f32[2,2,384,384]{3,2,1,0:T(8,128)S(1)} %copy-done.1, f32[2,2,2,64,384]{4,3,2,1,0:T(8,128)S(1)} %get-tuple-element.9.row_bands, f32[2,2,2,128,128]{4,3,2,1,0:T(8,128)S(1)} %get-tuple-element.10.col_bands, f32[3,2,256,256]{3,2,1,0:T(8,128)S(1)} %copy-done.2, ...), custom_call_target="tpu_custom_call" | custom-call | tf_op jit(solution)/shard_map/pallas_call | solution.py:563
Async XLA Ops:
  0.6 16.5 %copy-start.3 = (bf16[6,2,256,256]{3,2,1,0:T(8,128)(2,1)S(1)}, bf16[6,2,256,256]{3,2,1,0:T(8,128)(2,1)}, u32[]{:S(2)}) copy-start(bf16[6,2,256,256]{3,2,1,0:T(8,128)(2,1)} %constant.2.clone.tab) | copy-start | bytes 4718596
  0.6 16.5 %copy-start.2 = (f32[3,2,256,256]{3,2,1,0:T(8,128)S(1)}, f32[3,2,256,256]{3,2,1,0:T(8,128)}, u32[]{:S(2)}) copy-start(f32[3,2,256,256]{3,2,1,0:T(8,128)} %probe.3) | copy-start | bytes 4718596
  0.7 1.4 %copy-start.4 = (f32[2,2,256,256]{3,2,1,0:T(8,128)S(1)}, f32[2,2,256,256]{3,2,1,0:T(8,128)}, u32[]{:S(2)}) copy-start(f32[2,2,256,256]{3,2,1,0:T(8,128)} %field.1) | copy-start | bytes 3145732
  2.0 15.1 %copy-start.6 = (s32[1,1,2,2]{3,2,1,0:T(2,128)S(1)}, s32[1,1,2,2]{3,2,1,0:T(2,128)}, u32[]{:S(2)}) copy-start(s32[1,1,2,2]{3,2,1,0:T(2,128)} %offs.1) | copy-start | bytes 52
  15.7 1.4 %copy-start = (f32[2,2,384,384]{3,2,1,0:T(8,128)}, f32[2,2,384,384]{3,2,1,0:T(8,128)S(1)}, u32[]{:S(2)}) copy-start(f32[2,2,384,384]{3,2,1,0:T(8,128)S(1)} %shard_map.68.ext) | copy-start | bytes 7077892
  17.1 1.0 %copy-start.5 = (f32[1,1,2,256,256]{4,3,2,1,0:T(8,128)S(1)}, f32[1,1,2,256,256]{4,3,2,1,0:T(8,128)}, u32[]{:S(2)}) copy-start(f32[1,1,2,256,256]{4,3,2,1,0:T(8,128)} %meas.1) | copy-start | bytes 1572868
  48.3 44.5 %copy-start.1 = (f32[2,2,384,384]{3,2,1,0:T(8,128)S(1)}, f32[2,2,384,384]{3,2,1,0:T(8,128)}, u32[]{:S(2)}) copy-start(f32[2,2,384,384]{3,2,1,0:T(8,128)} %get-tuple-element.7.ext) | copy-start | bytes 7077892

commit v3 on v2

--- a/solution.py
+++ b/solution.py
@@ -452,40 +452,46 @@
 
     for m in range(modes):
         begin(m, 0)
-    start(to_high)
-    start(to_low)
     for m in range(modes):
         finish(m, 0)
         begin(m, 1)
-    arrive(to_high, row > 0, row_bands.at[0])
-    arrive(to_low, row < rows_total - 1, row_bands.at[1])
-    lane = lax.broadcasted_iota(jnp.int32, (size // 2, 128), 1)
-    for l in range(layers):
-        for c in range(2):
-            for slot, at in ((0, wide - 128), (1, 0)):
-                cut = pl.ds(at, 128)
-                half = size // 2
-                top = jnp.concatenate([
-                    ext[l, c, pl.ds(HALO, HALO), cut] + row_bands[0, l, c, :, cut],
-                    ext[l, c, pl.ds(2 * HALO, half - HALO), cut],
-                ], axis=0)
-                bottom = jnp.concatenate([
-                    ext[l, c, pl.ds(HALO + half, half - HALO), cut],
-                    ext[l, c, pl.ds(size, HALO), cut] + row_bands[1, l, c, :, cut],
-                ], axis=0)
-                if slot == 0:
-                    top = pltpu.roll(top, HALO, 1)
-                else:
-                    bottom = pltpu.roll(bottom, HALO, 1)
-                packed[slot, l, c] = halves(top, bottom, lane)
-    start(right)
-    start(left)
-    for wave in range(modes + 4):
+    start(to_high)
+    start(to_low)
+
+    def pack():
+        arrive(to_high, row > 0, row_bands.at[0])
+        arrive(to_low, row < rows_total - 1, row_bands.at[1])
+        lane = lax.broadcasted_iota(jnp.int32, (size // 2, 128), 1)
+        for l in range(layers):
+            for c in range(2):
+                for slot, at in ((0, wide - 128), (1, 0)):
+                    cut = pl.ds(at, 128)
+                    half = size // 2
+                    top = jnp.concatenate([
+                        ext[l, c, pl.ds(HALO, HALO), cut] + row_bands[0, l, c, :, cut],
+                        ext[l, c, pl.ds(2 * HALO, half - HALO), cut],
+                    ], axis=0)
+                    bottom = jnp.concatenate([
+                        ext[l, c, pl.ds(HALO + half, half - HALO), cut],
+                        ext[l, c, pl.ds(size, HALO), cut] + row_bands[1, l, c, :, cut],
+                    ], axis=0)
+                    if slot == 0:
+                        top = pltpu.roll(top, HALO, 1)
+                    else:
+                        bottom = pltpu.roll(bottom, HALO, 1)
+                    packed[slot, l, c] = halves(top, bottom, lane)
+
+    for wave in range(modes + 3):
         for m in range(modes):
             s = 1 + wave - m
             if 1 <= s <= 4:
                 finish(m, s)
                 begin(m, s + 1)
+        if wave == modes - 1:
+            pack()
+        if wave == modes:
+            start(right)
+            start(left)
     for m in range(modes):
         finish(m, 5)
     arrive(right, col > 0, col_bands.at[0])

time: 97.2 us -> 91.1 us (0.937)
  Pallas kernels: 91.6 us -> 85.8 us
    pallas_call x1, Pallas kernels: 44.5 us -> 38.7 us  [exchange(): pl.pallas_call(functools.partial(exchange_kernel, nx, nc), out_shape=(jax...]
where the time goes in v3:
time: 91.1 us; the launch traced here: 90.3 us
  Pallas kernels  85.8 us (94%)
  local copies, waits for them, and re-layouts  3.83 us (4%)
    pallas_call x1, Pallas kernels, exchange(): pl.pallas_call(functools.partial(exchange_kernel, nx, nc), out_shape=(jax...  38.7 us
    pallas_call x1, Pallas kernels, gradients(): pl.pallas_call(gradient_kernel, out_shape=(jax.ShapeDtypeStruct(extended....  30.1 us
    pallas_call x1, Pallas kernels, with_halo(): pl.pallas_call(functools.partial(halo_kernel, lax.axis_size('row'), lax.a...  13.6 us
    unnamed x14, local copies, waits for them, and re-layouts  3.83 us
    pallas_call x1, Pallas kernels, last(): pl.pallas_call(last_kernel, out_shape=(jax.ShapeDtypeStruct(grad_shape, f...  3.36 us

profile of v3, /device:TPU:0, one launch (start us, length us, event | category | flops | bytes accessed | tf_op | source)
XLA Modules:
  0.0 90.3 jit_solution(7838590326811616608)
XLA Ops:
  0.6 0.0 copy-start.3
  0.6 0.0 copy-start.2
  0.7 0.0 copy-start.4
  0.7 1.4 %copy-done.4 = f32[2,2,256,256]{3,2,1,0:T(8,128)S(1)} copy-done((f32[2,2,256,256]{3,2,1,0:T(8,128)S(1)}, f32[2,2,256,256]{3,2,1,0:T(8,128)}, u32[]{:S(2)}) %copy-start.4) | copy-done | bytes 1048600
  2.0 0.0 copy-start.6
  2.0 13.6 %shard_map.68.ext = f32[2,2,384,384]{3,2,1,0:T(8,128)S(1)} custom-call(f32[2,2,256,256]{3,2,1,0:T(8,128)S(1)} %copy-done.4), custom_call_target="tpu_custom_call" | custom-call | tf_op jit(solution)/shard_map/pallas_call | solution.py:310
  15.7 0.0 copy-start
  15.7 1.4 %copy-done = f32[2,2,384,384]{3,2,1,0:T(8,128)} copy-done((f32[2,2,384,384]{3,2,1,0:T(8,128)}, f32[2,2,384,384]{3,2,1,0:T(8,128)S(1)}, u32[]{:S(2)}) %copy-start) | copy-done | bytes 2359320
  17.1 0.0 copy-done.3
  17.1 0.0 copy-done.2
  17.1 0.0 copy-done.6
  17.1 0.0 copy-start.5
  17.1 1.0 %copy-done.5 = f32[1,1,2,256,256]{4,3,2,1,0:T(8,128)S(1)} copy-done((f32[1,1,2,256,256]{4,3,2,1,0:T(8,128)S(1)}, f32[1,1,2,256,256]{4,3,2,1,0:T(8,128)}, u32[]{:S(2)}) %copy-start.5) | copy-done | bytes 524312
  18.1 30.1 %shard_map.69 = (f32[2,2,384,384]{3,2,1,0:T(8,128)}, f32[3,2,256,256]{3,2,1,0:T(8,128)S(1)}) custom-call(s32[1,1,2,2]{3,2,1,0:T(2,128)S(1)} %copy-done.6, f32[2,2,384,384]{3,2,1,0:T(8,128)} %copy-done, f32[3,2,256,256]{3,2,1,0:T(8,128)S(1)} %copy-done.2, f32[1,1,2,256,256]{4,3,2,1,0:T(8,128)S(1)} %copy-done.5, bf16[6,2,256,256]{3,2,1,0:T(8,128)(2,1)S(1)} %copy-done.3), custom_call_target="tpu_custom_call" | custom-call | tf_op jit(solution)/shard_map/pallas_call | solution.py:177
  48.3 0.0 copy-start.1
  48.3 38.7 %shard_map.70 = (f32[3,2,256,256]{3,2,1,0:T(8,128)S(1)}, f32[2,2,2,64,384]{4,3,2,1,0:T(8,128)S(1)}, f32[2,2,2,128,128]{4,3,2,1,0:T(8,128)S(1)}) custom-call(f32[2,2,384,384]{3,2,1,0:T(8,128)} %get-tuple-element.7.ext, f32[3,2,256,256]{3,2,1,0:T(8,128)S(1)} %get-tuple-element.8.pgrad), custom_call_target="tpu_custom_call" | custom-call | tf_op jit(solution)/shard_map/pallas_call | solution.py:516
  87.0 0.0 copy-done.1
  87.0 3.4 %shard_map.71 = (f32[2,2,256,256]{3,2,1,0:T(8,128)}, f32[3,2,256,256]{3,2,1,0:T(8,128)}) custom-call(f32[2,2,384,384]{3,2,1,0:T(8,128)S(1)} %copy-done.1, f32[2,2,2,64,384]{4,3,2,1,0:T(8,128)S(1)} %get-tuple-element.9.row_bands, f32[2,2,2,128,128]{4,3,2,1,0:T(8,128)S(1)} %get-tuple-element.10.col_bands, f32[3,2,256,256]{3,2,1,0:T(8,128)S(1)} %copy-done.2, ...), custom_call_target="tpu_custom_call" | custom-call | tf_op jit(solution)/shard_map/pallas_call | solution.py:569
Async XLA Ops:
  0.6 16.5 %copy-start.3 = (bf16[6,2,256,256]{3,2,1,0:T(8,128)(2,1)S(1)}, bf16[6,2,256,256]{3,2,1,0:T(8,128)(2,1)}, u32[]{:S(2)}) copy-start(bf16[6,2,256,256]{3,2,1,0:T(8,128)(2,1)} %constant.2.clone.tab) | copy-start | bytes 4718596
  0.6 16.5 %copy-start.2 = (f32[3,2,256,256]{3,2,1,0:T(8,128)S(1)}, f32[3,2,256,256]{3,2,1,0:T(8,128)}, u32[]{:S(2)}) copy-start(f32[3,2,256,256]{3,2,1,0:T(8,128)} %probe.3) | copy-start | bytes 4718596
  0.7 1.4 %copy-start.4 = (f32[2,2,256,256]{3,2,1,0:T(8,128)S(1)}, f32[2,2,256,256]{3,2,1,0:T(8,128)}, u32[]{:S(2)}) copy-start(f32[2,2,256,256]{3,2,1,0:T(8,128)} %field.1) | copy-start | bytes 3145732
  2.0 15.1 %copy-start.6 = (s32[1,1,2,2]{3,2,1,0:T(2,128)S(1)}, s32[1,1,2,2]{3,2,1,0:T(2,128)}, u32[]{:S(2)}) copy-start(s32[1,1,2,2]{3,2,1,0:T(2,128)} %offs.1) | copy-start | bytes 52
  15.7 1.4 %copy-start = (f32[2,2,384,384]{3,2,1,0:T(8,128)}, f32[2,2,384,384]{3,2,1,0:T(8,128)S(1)}, u32[]{:S(2)}) copy-start(f32[2,2,384,384]{3,2,1,0:T(8,128)S(1)} %shard_map.68.ext) | copy-start | bytes 7077892
  17.1 1.0 %copy-start.5 = (f32[1,1,2,256,256]{4,3,2,1,0:T(8,128)S(1)}, f32[1,1,2,256,256]{4,3,2,1,0:T(8,128)}, u32[]{:S(2)}) copy-start(f32[1,1,2,256,256]{4,3,2,1,0:T(8,128)} %meas.1) | copy-start | bytes 1572868
  48.3 38.7 %copy-start.1 = (f32[2,2,384,384]{3,2,1,0:T(8,128)S(1)}, f32[2,2,384,384]{3,2,1,0:T(8,128)}, u32[]{:S(2)}) copy-start(f32[2,2,384,384]{3,2,1,0:T(8,128)} %get-tuple-element.7.ext) | copy-start | bytes 7077892

commit v4 on v3

--- a/solution.py
+++ b/solution.py
@@ -189,7 +189,7 @@
             pltpu.VMEM((size, size), f32),
             pltpu.VMEM((layers, 2, size, size), f32),
         ],
-        compiler_params=pltpu.CompilerParams(vmem_limit_bytes=48 << 20),
+        compiler_params=pltpu.CompilerParams(vmem_limit_bytes=28 << 20),
     )(offsets, extended, probe_modes, measured, tables)
 
 
@@ -322,7 +322,7 @@
             dma((6,)),
         ],
         compiler_params=pltpu.CompilerParams(
-            collective_id=1, has_side_effects=True, vmem_limit_bytes=32 << 20
+            collective_id=1, has_side_effects=True, vmem_limit_bytes=20 << 20
         ),
     )(field)
 
@@ -535,7 +535,7 @@
             dma((4,)),
         ],
         compiler_params=pltpu.CompilerParams(
-            collective_id=0, has_side_effects=True, vmem_limit_bytes=48 << 20
+            collective_id=0, has_side_effects=True, vmem_limit_bytes=28 << 20
         ),
     )(grad_ext, local_grad)
 
@@ -572,7 +572,7 @@
             jax.ShapeDtypeStruct(grad_shape, f32),
             jax.ShapeDtypeStruct(probe_modes.shape, f32),
         ),
-        compiler_params=pltpu.CompilerParams(vmem_limit_bytes=40 << 20),
+        compiler_params=pltpu.CompilerParams(vmem_limit_bytes=24 << 20),
     )(grad_ext, row_bands, col_bands, probe_modes, summed)
 
 

time: 91.1 us -> 85.1 us (0.934)
  Pallas kernels: 85.8 us -> 81.9 us
  local copies, waits for them, and re-layouts: 3.83 us -> 2.42 us
    pallas_call x1, Pallas kernels: 30.1 us -> 27.6 us  [gradients(): pl.pallas_call(gradient_kernel, out_shape=(jax.ShapeDtypeStruct(extended....]
    pallas_call x1, Pallas kernels: 38.7 us -> 37.3 us  [exchange(): pl.pallas_call(functools.partial(exchange_kernel, nx, nc), out_shape=(jax...]
    unnamed x14 -> x10, local copies, waits for them, and re-layouts: 3.83 us -> 2.42 us
where the time goes in v4:
time: 85.1 us; the launch traced here: 85 us
  Pallas kernels  81.9 us (96%)
  local copies, waits for them, and re-layouts  2.42 us (3%)
    pallas_call x1, Pallas kernels, exchange(): pl.pallas_call(functools.partial(exchange_kernel, nx, nc), out_shape=(jax...  37.3 us
    pallas_call x1, Pallas kernels, gradients(): pl.pallas_call(gradient_kernel, out_shape=(jax.ShapeDtypeStruct(extended....  27.6 us
    pallas_call x1, Pallas kernels, with_halo(): pl.pallas_call(functools.partial(halo_kernel, lax.axis_size('row'), lax.a...  13.6 us
    pallas_call x1, Pallas kernels, last(): pl.pallas_call(last_kernel, out_shape=(jax.ShapeDtypeStruct(grad_shape, f...  3.4 us
    unnamed x10, local copies, waits for them, and re-layouts  2.42 us

profile of v4, /device:TPU:0, one launch (start us, length us, event | category | flops | bytes accessed | tf_op | source)
XLA Modules:
  0.0 85.0 jit_solution(360918642684559354)
XLA Ops:
  0.6 0.0 copy-start.1
  0.6 0.0 copy-start
  0.7 0.0 copy-start.2
  0.7 1.4 %copy-done.2 = f32[2,2,256,256]{3,2,1,0:T(8,128)S(1)} copy-done((f32[2,2,256,256]{3,2,1,0:T(8,128)S(1)}, f32[2,2,256,256]{3,2,1,0:T(8,128)}, u32[]{:S(2)}) %copy-start.2) | copy-done | bytes 1048600
  2.0 0.0 copy-start.4
  2.0 13.6 %shard_map.68.ext = f32[2,2,384,384]{3,2,1,0:T(8,128)S(1)} custom-call(f32[2,2,256,256]{3,2,1,0:T(8,128)S(1)} %copy-done.2), custom_call_target="tpu_custom_call" | custom-call | tf_op jit(solution)/shard_map/pallas_call | solution.py:310
  15.7 0.0 copy-done.1
  15.7 0.0 copy-done
  15.7 0.0 copy-done.4
  15.7 0.0 copy-start.3
  15.7 1.0 %copy-done.3 = f32[1,1,2,256,256]{4,3,2,1,0:T(8,128)S(1)} copy-done((f32[1,1,2,256,256]{4,3,2,1,0:T(8,128)S(1)}, f32[1,1,2,256,256]{4,3,2,1,0:T(8,128)}, u32[]{:S(2)}) %copy-start.3) | copy-done | bytes 524312
  16.8 27.6 %shard_map.69 = (f32[2,2,384,384]{3,2,1,0:T(8,128)S(1)}, f32[3,2,256,256]{3,2,1,0:T(8,128)S(1)}) custom-call(s32[1,1,2,2]{3,2,1,0:T(2,128)S(1)} %copy-done.4, f32[2,2,384,384]{3,2,1,0:T(8,128)S(1)} %shard_map.68.ext, f32[3,2,256,256]{3,2,1,0:T(8,128)S(1)} %copy-done, f32[1,1,2,256,256]{4,3,2,1,0:T(8,128)S(1)} %copy-done.3, bf16[6,2,256,256]{3,2,1,0:T(8,128)(2,1)S(1)} %copy-done.1), custom_call_target="tpu_custom_call" | custom-call | tf_op jit(solution)/shard_map/pallas_call | solution.py:177
  44.3 37.3 %shard_map.70 = (f32[3,2,256,256]{3,2,1,0:T(8,128)S(1)}, f32[2,2,2,64,384]{4,3,2,1,0:T(8,128)S(1)}, f32[2,2,2,128,128]{4,3,2,1,0:T(8,128)S(1)}) custom-call(f32[2,2,384,384]{3,2,1,0:T(8,128)S(1)} %get-tuple-element.7.ext, f32[3,2,256,256]{3,2,1,0:T(8,128)S(1)} %get-tuple-element.8.pgrad), custom_call_target="tpu_custom_call" | custom-call | tf_op jit(solution)/shard_map/pallas_call | solution.py:516
  81.6 3.4 %shard_map.71 = (f32[2,2,256,256]{3,2,1,0:T(8,128)}, f32[3,2,256,256]{3,2,1,0:T(8,128)}) custom-call(f32[2,2,384,384]{3,2,1,0:T(8,128)S(1)} %get-tuple-element.7.ext, f32[2,2,2,64,384]{4,3,2,1,0:T(8,128)S(1)} %get-tuple-element.9.row_bands, f32[2,2,2,128,128]{4,3,2,1,0:T(8,128)S(1)} %get-tuple-element.10.col_bands, f32[3,2,256,256]{3,2,1,0:T(8,128)S(1)} %copy-done, ...), custom_call_target="tpu_custom_call" | custom-call | tf_op jit(solution)/shard_map/pallas_call | solution.py:569
Async XLA Ops:
  0.6 15.1 %copy-start.1 = (bf16[6,2,256,256]{3,2,1,0:T(8,128)(2,1)S(1)}, bf16[6,2,256,256]{3,2,1,0:T(8,128)(2,1)}, u32[]{:S(2)}) copy-start(bf16[6,2,256,256]{3,2,1,0:T(8,128)(2,1)} %constant.2.clone.tab) | copy-start | bytes 4718596
  0.6 15.1 %copy-start = (f32[3,2,256,256]{3,2,1,0:T(8,128)S(1)}, f32[3,2,256,256]{3,2,1,0:T(8,128)}, u32[]{:S(2)}) copy-start(f32[3,2,256,256]{3,2,1,0:T(8,128)} %probe.3) | copy-start | bytes 4718596
  0.7 1.4 %copy-start.2 = (f32[2,2,256,256]{3,2,1,0:T(8,128)S(1)}, f32[2,2,256,256]{3,2,1,0:T(8,128)}, u32[]{:S(2)}) copy-start(f32[2,2,256,256]{3,2,1,0:T(8,128)} %field.1) | copy-start | bytes 3145732
  2.0 13.7 %copy-start.4 = (s32[1,1,2,2]{3,2,1,0:T(2,128)S(1)}, s32[1,1,2,2]{3,2,1,0:T(2,128)}, u32[]{:S(2)}) copy-start(s32[1,1,2,2]{3,2,1,0:T(2,128)} %offs.1) | copy-start | bytes 52
  15.7 1.0 %copy-start.3 = (f32[1,1,2,256,256]{4,3,2,1,0:T(8,128)S(1)}, f32[1,1,2,256,256]{4,3,2,1,0:T(8,128)}, u32[]{:S(2)}) copy-start(f32[1,1,2,256,256]{4,3,2,1,0:T(8,128)} %meas.1) | copy-start | bytes 1572868
